TPU v7x, 32 devices: a whole 2x2x4 slice. The times are simulated.
32 devices in a mesh: groups: 2 (over x), tp: 16 (over z, y, core).
Axes of the slice: x: 2, y: 2, z: 4, core: 2. Of those that a mesh axis runs over, the one named last changes fastest.
Arguments:
- hidden: bfloat16 [256, 28672], P('groups', 'tp'), parts along dimension 0, may hold values from -6 to 6
- down_weight: bfloat16 [28672, 8192], P('tp'), may hold values from -0.046875 to 0.046875
- adapter_down_weight: bfloat16 [16, 64, 28672], P('tp'), may hold values from -0.03125 to 0.03125
- adapter_up_weight: bfloat16 [16, 64, 8192], P('tp'), may hold values from -0.75 to 0.75
- row_adapter_ids: int32 [256], P('groups'), parts along dimension 0, may hold values from 0 to 15, as said below
- adapter_holder: int32 [16], replicated, may hold values from 0 to 15, each once
Outputs:
- mixed: bfloat16 [256, 8192], P('groups', 'tp'), parts along dimension 0
There are 2 independent parts, one for each index of `groups`. A program takes and returns all parts, laid end to end along the dimension named above; an argument that names none is the same for every part. Nothing has to cross between parts.
Inputs may be any that keep to these rules, and one draw needn't show every extreme that they name: `row_adapter_ids`: exactly 24 rows name one adapter, and no adapter is named by more than 24 rows.
All inputs are finite; a program needn't handle non-finite values.
Results may differ from a plain program's by a relative error of at most 0.0039.
Values may be sent and summed in bfloat16 or wider, within the bound.
A program may use at most 128 MiB of HBM per device.

v0:
```python
import jax
import jax.numpy as jnp
from jax import lax
from jax.sharding import PartitionSpec as P

CAP = 24


def local(
    hidden, down_weight, adapter_down_weight, adapter_up_weight, row_adapter_ids, adapter_holder
):
    parts = lax.axis_size("tp")
    rows = hidden.shape[0]
    holder_device = adapter_holder[row_adapter_ids]
    owners = jnp.arange(parts, dtype=jnp.int32)
    onehot = (holder_device[:, None] == owners[None, :]).astype(jnp.int32)
    within = jnp.sum(jnp.cumsum(onehot, axis=0) * onehot, axis=1) - 1
    row_ids = jnp.arange(rows, dtype=jnp.int32)
    table = jnp.full((parts, CAP), rows, jnp.int32).at[holder_device, within].set(row_ids)
    outgoing = jnp.take(hidden, table, axis=0, mode="fill", fill_value=0)
    reduced_state = jnp.einsum(
        "sf,rf->sr",
        lax.all_to_all(outgoing, "tp", split_axis=0, concat_axis=2, tiled=True)[0],
        adapter_down_weight[0],
        preferred_element_type=jnp.float32,
    ).astype(jnp.bfloat16)
    adapter_row_outputs = jnp.dot(
        reduced_state, adapter_up_weight[0], preferred_element_type=jnp.float32
    )[None]
    partial_sum = jnp.dot(hidden, down_weight, preferred_element_type=jnp.float32)
    summed = lax.psum_scatter(partial_sum, "tp", scatter_dimension=1, tiled=True)
    delivered_rows = lax.all_to_all(
        adapter_row_outputs, "tp", split_axis=2, concat_axis=0, tiled=True
    )
    flat = delivered_rows.reshape(parts * CAP, delivered_rows.shape[2])
    back = jnp.take(flat, holder_device * CAP + within, axis=0)
    summed = summed + back
    return summed.astype(jnp.bfloat16)


def solution(mesh):
    return jax.shard_map(
        local,
        mesh=mesh,
        in_specs=(
            P("groups", "tp"),
            P("tp", None),
            P("tp", None, None),
            P("tp", None, None),
            P("groups"),
            P(),
        ),
        out_specs=P("groups", "tp"),
        check_vma=False,
    )
```

profile of v0, /device:TPU:0, one launch (start us, length us, event | category | flops | bytes accessed | tf_op | source)
XLA Modules:
  0.0 201.2 jit_solution(13948099085408538627)
XLA Ops:
  6.5 0.0 copy-start
  6.5 0.0 reduce-scatter.2.cloned.1.call-start
  6.5 15.5 %fusion.14 = f32[128,8192]{1,0:T(8,128)} fusion(bf16[128,1792]{1,0:T(8,128)(2,1)} %param.6, bf16[1792,8192]{1,0:T(8,128)(2,1)} %param.7), kind=kOutput, calls=%fused_computation.48 | convolution fusion | flops 3758096384 | bytes 34013184 | tf_op jit(solution)/shard_map/dot_general | solution.py:30
  22.0 0.0 copy-start.2
  22.0 0.0 copy-start.3
  22.0 0.0 copy-start.1
  22.0 0.0 reduce-scatter.2.cloned.1.call-update
  22.1 0.6 copy-done.2
  22.7 0.7 fusion.13
  23.4 0.0 copy-done.3
  23.4 10.0 %compare_select_fusion.6 = s32[128]{0:T(128)S(1)} fusion(s32[128]{0:T(128)S(1)} %copy-done.3, s32[]{:T(128)} %bitcast, s32[]{:T(128)} %bitcast.1, s32[]{:T(128)} %bitcast.2, s32[]{:T(128)} %bitcast.3, s32[]{:T(128)} %bitcast.4, s32[]{:T(128)} %bitcast.5, s32[]{:T(128)} %bitcast.6, s32[]{:T(128)} %bitcast.7, s32[]{:T(128)} %bitcast.8, s32[]{:T(128)} %bitcast.9, ...), kind=kLoop, calls=%fused_computation.23 | loop fusion | flops 4224 | bytes 1088 | tf_op jit(solution)/shard_map/gather | solution.py:14
  33.4 0.1 fusion.9
  33.5 0.2 reduce_window_sum.11
  33.7 0.2 select_reduce_fusion
  33.9 10.1 %fusion.11 = (s32[128]{0:T(128)S(1)}, s32[128]{0:T(128)S(1)}) fusion(s32[128]{0:T(128)S(1)} %select_reduce_fusion, s32[]{:T(128)} %bitcast.15, s32[]{:T(128)} %bitcast.14, s32[]{:T(128)} %bitcast.13, s32[]{:T(128)} %bitcast.12, s32[]{:T(128)} %bitcast.11, s32[]{:T(128)} %bitcast.10, s32[]{:T(128)} %bitcast.9, s32[]{:T(128)} %bitcast.8, s32[]{:T(128)} %bitcast.7, ...), kind=kLoop, calls=%fused_computation.42 | loop fusion | flops 6912 | bytes 2112 | tf_op jit(solution)/shard_map/jit(_take)/jit(_where)/select_n | solution.py:36
  43.9 7.0 %scatter_fusion = s32[16,24]{1,0:T(8,128)S(1)} fusion(s32[16,24]{1,0:T(8,128)S(1)} %broadcast_in_dim.37, s32[128]{0:T(128)S(1)} %get-tuple-element.6, s32[128]{0:T(128)S(1)} %iota.7), kind=kCustom, calls=%fused_computation.2 | custom fusion | bytes 2560 | tf_op jit(solution)/shard_map/scatter | solution.py:19
  51.0 0.1 reshape.99
  51.1 0.0 copy-done.1
  51.1 2.4 %gather_fusion = bf16[384,1792]{1,0:T(8,128)(2,1)S(1)} fusion(bf16[128,1792]{1,0:T(8,128)(2,1)S(1)} %copy-done.1, s32[1024]{0:T(1024)S(1)} %pad_clamp_fusion.1), kind=kCustom, calls=%fused_computation | custom fusion | bytes 2754048 | tf_op jit(solution)/shard_map/jit(_take)/gather | solution.py:20
  53.5 0.2 broadcast_select_fusion
  53.6 49.8 %all_to_all.30 = bf16[16,24,1792]{2,1,0:T(8,128)(2,1)S(1)} all-to-all(bf16[16,24,1792]{2,1,0:T(8,128)(2,1)S(1)} %broadcast_select_fusion), channel_id=1, replica_groups=mesh['groups'=2,'tp'=16] {'tp'}, dimensions={0} | all-to-all | bytes 2752512 | tf_op jit(solution)/shard_map/all_to_all | solution.py:23
  103.5 0.1 copy.14
  103.6 0.0 copy-done
  103.6 6.8 %fusion.6 = f32[24,8192]{0,1:T(8,128)} fusion(bf16[24,28672]{1,0:T(8,128)(2,1)S(1)} %bitcast.72, bf16[1,64,28672]{2,1,0:T(8,128)(2,1)} %param.8, bf16[1,64,8192]{2,1,0:T(8,128)(2,1)S(1)} %copy-done), kind=kOutput, calls=%fused_computation.7 | convolution fusion | flops 113247744 | bytes 6881280 | tf_op jit(solution)/shard_map/dot_general | solution.py:27
  110.4 0.6 broadcast.352
  111.0 38.4 %reduce = f32[8192,24]{1,0:T(8,128)} reduce(f32[8192,1,24]{2,1,0:T(1,128)} %bitcast.70, f32[]{:T(128)} %broadcast.352), dimensions={1}, to_apply=%bitcast.63.reduce_sub_computation | reduce | bytes 1572868
  149.4 5.4 %reshape.122 = f32[16,1,12288]{2,1,0:T(1,128)} reshape(f32[8192,24]{1,0:T(8,128)} %reduce) | data formatting | bytes 1572864
  154.7 4.0 %all-to-all-start.1 = ((f32[16,1,12288]{2,1,0:T(1,128)}), f32[16,1,12288]{2,1,0:T(1,128)S(1)}, u32[]{:S(2)}, u32[]{:S(2)}) async-start(f32[16,1,12288]{2,1,0:T(1,128)} %reshape.122), calls=%async_computation.2 | async-start | bytes 1572864 | tf_op jit(solution)/shard_map/all_to_all | solution.py:32
  158.8 10.0 %compare_and_fusion.1 = pred[128]{0:T(512)(128)(4,1)S(1)} fusion(s32[128]{0:T(128)S(1)} %select_reduce_fusion, s32[]{:T(128)} %bitcast.15, s32[]{:T(128)} %bitcast.14, s32[]{:T(128)} %bitcast.13, s32[]{:T(128)} %bitcast.12, s32[]{:T(128)} %bitcast.11, s32[]{:T(128)} %bitcast.10, s32[]{:T(128)} %bitcast.9, s32[]{:T(128)} %bitcast.8, s32[]{:T(128)} %bitcast.7, ...), kind=kLoop, calls=%fused_computation.38 | loop fusion | flops 5376 | bytes 1216 | tf_op jit(solution)/shard_map/jit(_take)/and | solution.py:36
  168.8 8.7 %all-to-all-done.1 = f32[16,1,12288]{2,1,0:T(1,128)S(1)} async-done(((f32[16,1,12288]{2,1,0:T(1,128)}), f32[16,1,12288]{2,1,0:T(1,128)S(1)}, u32[]{:S(2)}, u32[]{:S(2)}) %all-to-all-start.1) | async-done | bytes 786464 | tf_op jit(solution)/shard_map/all_to_all | solution.py:32
  177.5 2.5 %reduce.1 = f32[16,12288]{1,0:T(8,128)S(1)} reduce(f32[16,1,12288]{2,1,0:T(1,128)S(1)} %all-to-all-done.1, f32[]{:T(128)} %broadcast.352), dimensions={1}, to_apply=%all_to_all.25.reduce_sub_computation | reduce | bytes 1572868 | tf_op jit(solution)/shard_map/all_to_all | solution.py:32
  180.0 9.1 %reshape.123 = f32[8192,1,24]{2,1,0:T(1,128)} reshape(f32[16,12288]{1,0:T(8,128)S(1)} %reduce.1) | data formatting | bytes 1572864
  189.0 2.8 %copy.13 = f32[1,24,16,512]{3,1,2,0:T(8,128)S(1)} copy(f32[1,24,16,512]{1,3,2,0:T(8,128)} %bitcast.69) | data formatting | bytes 1572864 | tf_op jit(solution)/shard_map/all_to_all | solution.py:32
  191.8 0.8 gather_fusion.1
  192.6 0.0 reduce-scatter.2.cloned.1.call-done
  192.6 1.7 add_convert_fusion
  (6 shorter events, 0.0 us)
Async XLA Ops:
  6.5 97.0 %copy-start = (bf16[1,64,8192]{2,1,0:T(8,128)(2,1)S(1)}, bf16[1,64,8192]{2,1,0:T(8,128)(2,1)}, u32[]{:S(2)}) copy-start(bf16[1,64,8192]{2,1,0:T(8,128)(2,1)} %param.9) | copy-start | bytes 3145732
  6.5 186.1 %reduce-scatter.2.cloned.1.call-start = ((), (), s32[]{:S(2)}) async-start(), calls=%async_computation.3 | async-start | bytes 4456448 | tf_op jit(solution)/shard_map/reduce_scatter | solution.py:31
  22.0 0.7 copy-start.2
  22.0 1.4 copy-start.3
  22.0 29.0 %copy-start.1 = (bf16[128,1792]{1,0:T(8,128)(2,1)S(1)}, bf16[128,1792]{1,0:T(8,128)(2,1)}, u32[]{:S(2)}) copy-start(bf16[128,1792]{1,0:T(8,128)(2,1)} %param.6) | copy-start | bytes 1376260
  154.7 22.8 %all-to-all-start.1 = ((f32[16,1,12288]{2,1,0:T(1,128)}), f32[16,1,12288]{2,1,0:T(1,128)S(1)}, u32[]{:S(2)}, u32[]{:S(2)}) async-start(f32[16,1,12288]{2,1,0:T(1,128)} %reshape.122), calls=%async_computation.2 | async-start | bytes 1572864 | tf_op jit(solution)/shard_map/all_to_all | solution.py:32
Sparse Core Ops, SparseCore 0:
  22.2 93.8 reduce-scatter.1
where the time goes:
time: 202 us; the launch traced here: 201 us
  other arithmetic  73.3 us (36%)
  blocking collectives  49.8 us (25%)
  local copies, waits for them, and re-layouts  29.5 us (15%)
  matrix products  22.3 us (11%)
  between operations  13.6 us (7%)
  waiting for transfers between devices  8.69 us (4%)
  starting transfers between devices  4.05 us (2%)
    all_to_all x1, blocking collectives, local(): lax.all_to_all(outgoing, 'tp', split_axis=0, concat_axis=2, tiled=True)[0]  49.8 us
    unnamed x1, other arithmetic  38.4 us
    unnamed x12, local copies, waits for them, and re-layouts  15.7 us
    dot_general x1, matrix products, local(): jnp.dot(hidden, down_weight, preferred_element_type=jnp.float32)  15.5 us
    select_n x1, other arithmetic, local(): back = jnp.take(flat, holder_device * CAP + within, axis=0)  10.1 us
    and x1, other arithmetic, local(): back = jnp.take(flat, holder_device * CAP + within, axis=0)  10 us
    gather x1, other arithmetic, local(): holder_device = adapter_holder[row_adapter_ids]  10 us
    all_to_all x1, waiting for transfers between devices, local(): lax.all_to_all(adapter_row_outputs, 'tp', split_axis=2, concat_axis=0, ti...  8.65 us
  transfers between devices with their start and end apart: 2, of which 1 were waited for; matrix products, arithmetic and copies ran while one was open for 53% of the time, Pallas kernels for 0%

commit v1 on v0

v1 whole, which is shorter than its diff:
```python
import functools

import jax
import jax.numpy as jnp
from jax import lax
from jax.experimental import pallas as pl
from jax.experimental.pallas import tpu as pltpu
from jax.sharding import PartitionSpec as P

CAP = 24
F32 = jnp.float32
BF16 = jnp.bfloat16
LEVEL = 4


def mm(a, b):
    return jnp.dot(a, b, preferred_element_type=F32)


def kernel(
    levels, hid, ids, holder, down_hbm, a_hbm, u_hbm, out,
    w, a, u, sel, pack, got, core_out, core_in, y_out, y_in, total,
    lora_out, lora_in, z_out, z_in,
    w_sem, a_sem, u_sem, pack_s, pack_r, core_s, core_r, y_s, y_r, lora_s, lora_r, z_s, z_r,
):
    parts = levels * LEVEL
    rows, depth = hid.shape
    half = depth // 2
    width = out.shape[1]
    me = lax.axis_index("tp")
    z, y, c = me // 4, (me // 2) % 2, me % 2

    def device(dz, dy, dc):
        return ((z + dz) % levels) * 4 + ((y + dy) % 2) * 2 + (c + dc) % 2

    def back(dz, dy, dc):
        return ((z + levels - dz) % levels) * 4 + ((y + dy) % 2) * 2 + (c + dc) % 2

    def feature(zz, dy, dc):
        block = zz * 4 + ((y + dy) % 2) * 2 + (c + dc) % 2
        return pl.ds(pl.multiple_of(block * width, 128), width)

    def send(src, dst, s, r, dev):
        return pltpu.make_async_remote_copy(
            src_ref=src, dst_ref=dst, send_sem=s, recv_sem=r,
            device_id={"tp": dev}, device_id_type=pl.DeviceIdType.MESH,
        )

    phases = [(1, 1), (1, 0), (0, 1), (0, 0)]

    def w_copy(p, zz):
        dy, dc = phases[p]
        return pltpu.make_async_copy(
            down_hbm.at[:, feature(zz, dy, dc)], w.at[p * levels + zz], w_sem.at[p * levels + zz]
        )

    barrier = pltpu.get_barrier_semaphore()
    offsets = [(k // 4, (k // 2) % 2, k % 2) for k in range(parts)]
    for k in range(1, parts):
        pl.semaphore_signal(
            barrier, inc=1, device_id={"tp": device(*offsets[k])},
            device_id_type=pl.DeviceIdType.MESH,
        )
    for p in range(4):
        for zz in range(levels):
            w_copy(p, zz).start()
    a_copy = pltpu.make_async_copy(a_hbm, a, a_sem)
    u_copy = pltpu.make_async_copy(u_hbm, u, u_sem)
    a_copy.start()
    u_copy.start()

    held = (holder[...] == lax.broadcasted_iota(jnp.int32, (parts, parts), 0)).astype(F32)
    named = (ids[...] == lax.broadcasted_iota(jnp.int32, (parts, rows), 0)).astype(F32)
    owned = mm(held.astype(BF16), named.astype(BF16))
    upto = (
        lax.broadcasted_iota(jnp.int32, (rows, rows), 0)
        <= lax.broadcasted_iota(jnp.int32, (rows, rows), 1)
    ).astype(F32)
    count = mm(owned.astype(BF16), upto.astype(BF16))
    slot = jnp.where(owned > 0.5, count - 1.0, -1.0).astype(jnp.int32)
    for o in range(parts):
        sel[o] = (
            slot[o : o + 1, :] == lax.broadcasted_iota(jnp.int32, (CAP, rows), 0)
        ).astype(F32)

    def pack_level(i, carry):
        s = sel[pl.ds(i * 4, 4)].reshape(4 * CAP, rows).astype(BF16)
        t = mm(s, hid[...])
        for j in range(4):
            r = t[j * CAP : (j + 1) * CAP]
            pack[i * 4 + j] = jnp.concatenate([r[:, :half], r[:, half:]], axis=0).astype(BF16)
        return carry

    lax.fori_loop(0, levels, pack_level, 0)
    pl.semaphore_wait(barrier, parts - 1)

    pack_copies = [None] * parts
    for k in list(range(parts - 1, 0, -1)):
        dev = device(*offsets[k])
        pack_copies[k] = send(pack.at[dev], got.at[k], pack_s.at[k], pack_r.at[k], dev)
        pack_copies[k].start()

    def core_copy(i):
        return send(core_out.at[i], core_in.at[i], core_s.at[i], core_r.at[i], device(0, 0, 1))

    def y_copy(i):
        return send(y_out.at[i], y_in.at[i], y_s.at[i], y_r.at[i], device(0, 1, 0))

    def product(p, zz):
        w_copy(p, zz).wait()
        return mm(hid[...], w[p * levels + zz])

    def to_core(base, p):
        def body(zz, carry):
            core_out[base + zz] = product(p, zz)
            core_copy(base + zz).start()
            return carry
        lax.fori_loop(0, levels, body, 0)

    def to_y(zz, carry):
        t = product(1, zz)
        core_copy(zz).wait_recv()
        y_out[zz] = (t + core_in[zz]).astype(BF16)
        y_copy(zz).start()
        return carry

    def keep(zz, carry):
        t = product(3, zz)
        core_copy(levels + zz).wait_recv()
        t = t + core_in[levels + zz]
        y_copy(zz).wait_recv()
        total[zz] = t + y_in[zz].astype(F32)
        return carry

    to_core(0, 0)
    lax.fori_loop(0, levels, to_y, 0)
    to_core(levels, 2)
    lax.fori_loop(0, levels, keep, 0)

    a_copy.wait()
    low = jnp.zeros((CAP, a.shape[0]), F32)
    for k in range(parts):
        src = back(*offsets[k])
        if k == 0:
            x = pack[me]
        else:
            pack_copies[k].wait_recv()
            x = got[k]
        at = pl.multiple_of(src * depth, 128)
        dims = (((1,), (1,)), ((), ()))
        t0 = lax.dot_general(x, a[:, pl.ds(at, half)], dims, preferred_element_type=F32)
        t1 = lax.dot_general(
            x, a[:, pl.ds(pl.multiple_of(at + half, 128), half)], dims, preferred_element_type=F32
        )
        low = low + t0[:CAP] + t1[CAP:]
    low = low.astype(BF16)

    u_copy.wait()
    lora_copies = [None] * LEVEL
    for k in (3, 2, 1, 0):
        dy, dc = k // 2, k % 2
        value = jnp.concatenate(
            [mm(low, u[:, feature(zz, dy, dc)]) for zz in range(levels)], axis=0
        ).astype(BF16)
        if k == 0:
            lora_in[0] = value
        else:
            lora_out[k] = value
            lora_copies[k] = send(
                lora_out.at[k], lora_in.at[k], lora_s.at[k], lora_r.at[k], device(0, dy, dc)
            )
            lora_copies[k].start()
    for k in (1, 2, 3):
        lora_copies[k].wait_recv()

    terms = lora_in[...].reshape(LEVEL * levels * CAP, width)
    places = [sel[back(0, k // 2, k % 2)] for k in range(LEVEL)]

    def summed(dz):
        zz = (z + dz) % levels
        place = jnp.concatenate(
            [jnp.where(zz == i, places[k], 0.0) for k in range(LEVEL) for i in range(levels)], axis=0
        ).astype(BF16)
        return total[zz] + lax.dot_general(
            place, terms, (((0,), (0,)), ((), ())), preferred_element_type=F32
        )

    z_copies = [None] * levels
    for dz in range(levels - 1, 0, -1):
        z_out[dz] = summed(dz).astype(BF16)
        z_copies[dz] = send(z_out.at[dz], z_in.at[dz], z_s.at[dz], z_r.at[dz], device(dz, 0, 0))
        z_copies[dz].start()
    result = summed(0)
    for dz in range(1, levels):
        z_copies[dz].wait_recv()
        result = result + z_in[dz].astype(F32)
    out[...] = result.astype(out.dtype)

    for k in range(1, parts):
        pack_copies[k].wait_send()
    for i in range(2 * levels):
        core_copy(i).wait_send()
    for i in range(levels):
        y_copy(i).wait_send()
    for k in (1, 2, 3):
        lora_copies[k].wait_send()
    for dz in range(1, levels):
        z_copies[dz].wait_send()


def fused(hidden, down_weight, adapter_down, adapter_up, ids, holder):
    parts = lax.axis_size("tp")
    levels = parts // LEVEL
    rows, depth = hidden.shape
    features = down_weight.shape[1]
    width = features // parts
    rank = adapter_down.shape[0]
    vmem = pl.BlockSpec(memory_space=pltpu.VMEM)
    anywhere = pl.BlockSpec(memory_space=pl.ANY)
    dma = pltpu.SemaphoreType.DMA
    return pl.pallas_call(
        functools.partial(kernel, levels),
        out_shape=jax.ShapeDtypeStruct((rows, width), BF16),
        in_specs=[vmem, vmem, vmem, anywhere, anywhere, anywhere],
        out_specs=vmem,
        scratch_shapes=[
            pltpu.VMEM((parts, depth, width), BF16),
            pltpu.VMEM(adapter_down.shape, BF16),
            pltpu.VMEM(adapter_up.shape, BF16),
            pltpu.VMEM((parts, CAP, rows), F32),
            pltpu.VMEM((parts, 2 * CAP, depth // 2), BF16),
            pltpu.VMEM((parts, 2 * CAP, depth // 2), BF16),
            pltpu.VMEM((2 * levels, rows, width), F32),
            pltpu.VMEM((2 * levels, rows, width), F32),
            pltpu.VMEM((levels, rows, width), BF16),
            pltpu.VMEM((levels, rows, width), BF16),
            pltpu.VMEM((levels, rows, width), F32),
            pltpu.VMEM((LEVEL, levels * CAP, width), BF16),
            pltpu.VMEM((LEVEL, levels * CAP, width), BF16),
            pltpu.VMEM((levels, rows, width), BF16),
            pltpu.VMEM((levels, rows, width), BF16),
            dma((parts,)), dma, dma,
            dma((parts,)), dma((parts,)),
            dma((2 * levels,)), dma((2 * levels,)),
            dma((levels,)), dma((levels,)),
            dma((LEVEL,)), dma((LEVEL,)),
            dma((levels,)), dma((levels,)),
        ],
        compiler_params=pltpu.CompilerParams(
            collective_id=0, has_side_effects=True, vmem_limit_bytes=60 * 1024 * 1024
        ),
        cost_estimate=pl.CostEstimate(
            flops=2 * rows * depth * features,
            bytes_accessed=2 * depth * features,
            transcendentals=0,
        ),
    )(hidden, ids.reshape(1, rows), holder.reshape(1, parts), down_weight, adapter_down, adapter_up)


def general(
    hidden, down_weight, adapter_down_weight, adapter_up_weight, row_adapter_ids, adapter_holder
):
    parts = lax.axis_size("tp")
    rows = hidden.shape[0]
    holder_device = adapter_holder[row_adapter_ids]
    owners = jnp.arange(parts, dtype=jnp.int32)
    onehot = (holder_device[:, None] == owners[None, :]).astype(jnp.int32)
    within = jnp.sum(jnp.cumsum(onehot, axis=0) * onehot, axis=1) - 1
    row_ids = jnp.arange(rows, dtype=jnp.int32)
    table = jnp.full((parts, CAP), rows, jnp.int32).at[holder_device, within].set(row_ids)
    outgoing = jnp.take(hidden, table, axis=0, mode="fill", fill_value=0)
    reduced_state = jnp.einsum(
        "sf,rf->sr",
        lax.all_to_all(outgoing, "tp", split_axis=0, concat_axis=2, tiled=True)[0],
        adapter_down_weight[0],
        preferred_element_type=F32,
    ).astype(BF16)
    mine = (holder_device == lax.axis_index("tp"))[:, None]
    low = jnp.where(mine, jnp.take(reduced_state, within, axis=0, mode="clip"), 0)
    partial_sum = mm(hidden, down_weight) + mm(low, adapter_up_weight[0])
    return lax.psum_scatter(partial_sum, "tp", scatter_dimension=1, tiled=True).astype(BF16)


def local(
    hidden, down_weight, adapter_down_weight, adapter_up_weight, row_adapter_ids, adapter_holder
):
    parts = lax.axis_size("tp")
    tiled = (
        parts % LEVEL == 0
        and hidden.shape[1] % 256 == 0
        and down_weight.shape[1] % (128 * parts) == 0
        and hidden.shape[0] == 128
        and hidden.shape[1] * down_weight.shape[1] <= 2**24
        and adapter_holder.shape[0] == parts
    )
    if tiled:
        return fused(
            hidden, down_weight, adapter_down_weight[0], adapter_up_weight[0],
            row_adapter_ids, adapter_holder,
        )
    return general(
        hidden, down_weight, adapter_down_weight, adapter_up_weight, row_adapter_ids, adapter_holder
    )


def solution(mesh):
    return jax.shard_map(
        local,
        mesh=mesh,
        in_specs=(
            P("groups", "tp"),
            P("tp", None),
            P("tp", None, None),
            P("tp", None, None),
            P("groups"),
            P(),
        ),
        out_specs=P("groups", "tp"),
        check_vma=False,
    )
```

time: 202 us -> 61.6 us (0.30)
  other arithmetic: 73.3 us -> 0 us
  Pallas kernels: 0 us -> 59.9 us
  blocking collectives: 49.8 us -> 0 us
  local copies, waits for them, and re-layouts: 29.5 us -> 1.57 us
  matrix products: 22.3 us -> 0 us
  between operations: 13.6 us -> 0.01 us
  waiting for transfers between devices: 8.69 us -> 0 us
  starting transfers between devices: 4.05 us -> 0 us
    pallas_call x0 -> x1, Pallas kernels: none -> 59.9 us  [fused(): pl.pallas_call(functools.partial(kernel, levels), out_shape=jax.ShapeDtyp...]
    all_to_all x1 -> x0, blocking collectives: 49.8 us -> none  [local(): lax.all_to_all(outgoing, 'tp', split_axis=0, concat_axis=2, tiled=True)[0]]
    unnamed x1 -> x0, other arithmetic: 38.4 us -> none
    dot_general x2 -> x0, matrix products: 22.3 us -> none  [the longest x1 15.5 us: local(): jnp.dot(hidden, down_weight, preferred_element_type=jnp.float32)]
    unnamed x12 -> x1, local copies, waits for them, and re-layouts: 15.7 us -> 1.57 us
    select_n x3 -> x0, other arithmetic: 10.2 us -> none  [the longest x1 10.1 us: local(): back = jnp.take(flat, holder_device * CAP + within, axis=0)]
    gather x3 -> x0, other arithmetic: 10 us -> none  [the longest x1 10 us: local(): holder_device = adapter_holder[row_adapter_ids]]
    and x2 -> x0, other arithmetic: 10 us -> none  [the longest x1 10 us: local(): back = jnp.take(flat, holder_device * CAP + within, axis=0)]
  transfers between devices with their start and end apart: 2 -> 0, of which waited for: 1 -> 0; matrix products, arithmetic and copies ran while one was open for 53% -> 0% of each run, Pallas kernels for 0% -> 0%
where the time goes in v1:
time: 61.6 us; the launch traced here: 61.5 us
  Pallas kernels  59.9 us (97%)
  local copies, waits for them, and re-layouts  1.57 us (3%)
    pallas_call x1, Pallas kernels, fused(): pl.pallas_call(functools.partial(kernel, levels), out_shape=jax.ShapeDtyp...  59.9 us
    unnamed x1, local copies, waits for them, and re-layouts  1.57 us

profile of v1, /device:TPU:0, one launch (start us, length us, event | category | flops | bytes accessed | tf_op | source)
XLA Modules:
  0.0 61.5 jit_solution(18217635457347491992)
XLA Ops:
  0.0 59.9 %shard_map.64 = bf16[128,512]{1,0:T(8,128)(2,1)} custom-call(bf16[128,1792]{1,0:T(8,128)(2,1)} %hid.1, s32[1,128]{1,0:T(1,128)} %bitcast.6, s32[1,16]{1,0:T(1,128)} %bitcast.7, bf16[1792,8192]{1,0:T(8,128)(2,1)} %down_hbm.1, bf16[64,28672]{1,0:T(8,128)(2,1)} %bitcast.4, bf16[64,8192]{1,0:T(8,128)(2,1)} %bitcast.5), custom_call_target="tpu_custom_call" | custom-call | flops 3758096384 | bytes 29360128 | tf_op jit(solution)/shard_map/pallas_call | solution.py:221
  59.9 1.6 %copy.8 = bf16[128,512]{1,0:T(8,128)(2,1)} copy(bf16[128,512]{1,0:T(8,128)(2,1)} %shard_map.64) | data formatting | bytes 262144

commit v2 on v1

--- a/solution.py
+++ b/solution.py
@@ -19,22 +19,28 @@
 
 def kernel(
     levels, hid, ids, holder, down_hbm, a_hbm, u_hbm, out,
-    w, a, u, sel, pack, got, core_out, core_in, y_out, y_in, total,
-    lora_out, lora_in, z_out, z_in,
-    w_sem, a_sem, u_sem, pack_s, pack_r, core_s, core_r, y_s, y_r, lora_s, lora_r, z_s, z_r,
+    w, a, u, sel, place, far, near_out, near_in, relay_out, relay_in, direct_out, direct_in,
+    core_out, core_in, y_out, y_in, total, lora_out, lora_in, z_out, z_in,
+    w_sem, a_sem, u_sem, far_s, far_r, near_s, near_r, relay_s, relay_r, direct_s, direct_r,
+    core_s, core_r, y_s, y_r, lora_s, lora_r, z_s, z_r,
 ):
     parts = levels * LEVEL
+    side = parts // 2
     rows, depth = hid.shape
-    half = depth // 2
+    relayed = far.shape[1]
     width = out.shape[1]
     me = lax.axis_index("tp")
     z, y, c = me // 4, (me // 2) % 2, me % 2
+    half, zin = z // 2, z % 2
 
     def device(dz, dy, dc):
         return ((z + dz) % levels) * 4 + ((y + dy) % 2) * 2 + (c + dc) % 2
 
     def back(dz, dy, dc):
         return ((z + levels - dz) % levels) * 4 + ((y + dy) % 2) * 2 + (c + dc) % 2
+
+    def inner(j):
+        return ((zin + j // 4) % 2) * 4 + ((y + (j // 2) % 2) % 2) * 2 + (c + j % 2) % 2
 
     def feature(zz, dy, dc):
         block = zz * 4 + ((y + dy) % 2) * 2 + (c + dc) % 2
@@ -83,22 +89,37 @@
             slot[o : o + 1, :] == lax.broadcasted_iota(jnp.int32, (CAP, rows), 0)
         ).astype(F32)
 
-    def pack_level(i, carry):
-        s = sel[pl.ds(i * 4, 4)].reshape(4 * CAP, rows).astype(BF16)
-        t = mm(s, hid[...])
-        for j in range(4):
-            r = t[j * CAP : (j + 1) * CAP]
-            pack[i * 4 + j] = jnp.concatenate([r[:, :half], r[:, half:]], axis=0).astype(BF16)
-        return carry
-
-    lax.fori_loop(0, levels, pack_level, 0)
     pl.semaphore_wait(barrier, parts - 1)
-
-    pack_copies = [None] * parts
-    for k in list(range(parts - 1, 0, -1)):
-        dev = device(*offsets[k])
-        pack_copies[k] = send(pack.at[dev], got.at[k], pack_s.at[k], pack_r.at[k], dev)
-        pack_copies[k].start()
+    far_copy = send(hid.at[:, pl.ds(0, relayed)], far, far_s, far_r, device(levels // 2, 0, 0))
+    far_copy.start()
+
+    def pack(first, groups, x, to):
+        def body(i, carry):
+            s = sel[pl.ds(first + i * 4, 4)].reshape(4 * CAP, rows).astype(BF16)
+            t = mm(s, x())
+            n = t.shape[1] // 2
+            for j in range(4):
+                r = t[j * CAP : (j + 1) * CAP]
+                to[i * 4 + j] = jnp.concatenate([r[:, :n], r[:, n:]], axis=0).astype(BF16)
+            return carry
+
+        lax.fori_loop(0, groups, body, 0)
+
+    pack(half * side, side // 4, lambda: hid[:, :relayed], near_out)
+    near_copies = [
+        send(near_out.at[inner(j)], near_in.at[j], near_s.at[j], near_r.at[j], half * side + inner(j))
+        for j in range(side)
+    ]
+    for j in range(side - 1, 0, -1):
+        near_copies[j].start()
+    pack(0, levels, lambda: hid[:, relayed:], direct_out)
+    direct_copies = [
+        send(direct_out.at[device(*offsets[k])], direct_in.at[k], direct_s.at[k], direct_r.at[k],
+             device(*offsets[k]))
+        for k in range(parts)
+    ]
+    for k in range(parts - 1, 0, -1):
+        direct_copies[k].start()
 
     def core_copy(i):
         return send(core_out.at[i], core_in.at[i], core_s.at[i], core_r.at[i], device(0, 0, 1))
@@ -135,75 +156,105 @@
     to_core(0, 0)
     lax.fori_loop(0, levels, to_y, 0)
     to_core(levels, 2)
+
+    far_copy.wait_recv()
+    pack(half * side, side // 4, lambda: far[...], relay_out)
+    relay_copies = [
+        send(relay_out.at[inner(j)], relay_in.at[j], relay_s.at[j], relay_r.at[j],
+             half * side + inner(j))
+        for j in range(side)
+    ]
+    for j in range(side - 1, 0, -1):
+        relay_copies[j].start()
+
     lax.fori_loop(0, levels, keep, 0)
 
+    level_sel = [sel[back(0, k // 2, k % 2)] for k in range(LEVEL)]
+    zeros = jnp.zeros((CAP, rows), F32)
+    for pos in range(2):
+        pieces = []
+        for s in level_sel:
+            pieces += [s, zeros] if pos == 0 else [zeros, s]
+        place[pos] = jnp.concatenate(pieces, axis=0).T.astype(BF16)
+
     a_copy.wait()
-    low = jnp.zeros((CAP, a.shape[0]), F32)
-    for k in range(parts):
-        src = back(*offsets[k])
-        if k == 0:
-            x = pack[me]
-        else:
-            pack_copies[k].wait_recv()
-            x = got[k]
-        at = pl.multiple_of(src * depth, 128)
+
+    def down_map(x, at):
+        n = x.shape[1]
         dims = (((1,), (1,)), ((), ()))
-        t0 = lax.dot_general(x, a[:, pl.ds(at, half)], dims, preferred_element_type=F32)
+        t0 = lax.dot_general(
+            x, a[:, pl.ds(pl.multiple_of(at, 128), n)], dims, preferred_element_type=F32
+        )
         t1 = lax.dot_general(
-            x, a[:, pl.ds(pl.multiple_of(at + half, 128), half)], dims, preferred_element_type=F32
-        )
-        low = low + t0[:CAP] + t1[CAP:]
+            x, a[:, pl.ds(pl.multiple_of(at + n, 128), n)], dims, preferred_element_type=F32
+        )
+        return t0[:CAP] + t1[CAP:]
+
+    low = down_map(near_out[inner(0)], me * depth)
+    low += down_map(direct_out[me], me * depth + relayed)
+    low += down_map(relay_out[inner(0)], ((1 - half) * side + inner(0)) * depth)
+    for j in range(1, side):
+        near_copies[j].wait_recv()
+        low += down_map(near_in[j], (half * side + inner(j)) * depth)
+    for k in range(1, parts):
+        direct_copies[k].wait_recv()
+        low += down_map(direct_in[k], back(*offsets[k]) * depth + relayed)
+    for j in range(1, side):
+        relay_copies[j].wait_recv()
+        low += down_map(relay_in[j], ((1 - half) * side + inner(j)) * depth)
     low = low.astype(BF16)
 
     u_copy.wait()
-    lora_copies = [None] * LEVEL
-    for k in (3, 2, 1, 0):
-        dy, dc = k // 2, k % 2
-        value = jnp.concatenate(
-            [mm(low, u[:, feature(zz, dy, dc)]) for zz in range(levels)], axis=0
-        ).astype(BF16)
-        if k == 0:
-            lora_in[0] = value
-        else:
-            lora_out[k] = value
-            lora_copies[k] = send(
-                lora_out.at[k], lora_in.at[k], lora_s.at[k], lora_r.at[k], device(0, dy, dc)
-            )
-            lora_copies[k].start()
-    for k in (1, 2, 3):
-        lora_copies[k].wait_recv()
-
-    terms = lora_in[...].reshape(LEVEL * levels * CAP, width)
-    places = [sel[back(0, k // 2, k % 2)] for k in range(LEVEL)]
-
-    def summed(dz):
-        zz = (z + dz) % levels
-        place = jnp.concatenate(
-            [jnp.where(zz == i, places[k], 0.0) for k in range(LEVEL) for i in range(levels)], axis=0
-        ).astype(BF16)
-        return total[zz] + lax.dot_general(
-            place, terms, (((0,), (0,)), ((), ())), preferred_element_type=F32
-        )
-
-    z_copies = [None] * levels
-    for dz in range(levels - 1, 0, -1):
-        z_out[dz] = summed(dz).astype(BF16)
-        z_copies[dz] = send(z_out.at[dz], z_in.at[dz], z_s.at[dz], z_r.at[dz], device(dz, 0, 0))
-        z_copies[dz].start()
-    result = summed(0)
+    steps = [(2, 3), (1, 0)]
+    lora_copies = {}
+    for piece, dzs in enumerate(steps):
+        for k in (3, 2, 1, 0):
+            dy, dc = k // 2, k % 2
+            value = jnp.concatenate(
+                [mm(low, u[:, feature((z + dz) % levels, dy, dc)]) for dz in dzs], axis=0
+            ).astype(BF16)
+            i = piece * LEVEL + k
+            if k == 0:
+                lora_in[i] = value
+            else:
+                lora_out[i] = value
+                lora_copies[i] = send(
+                    lora_out.at[i], lora_in.at[i], lora_s.at[i], lora_r.at[i], device(0, dy, dc)
+                )
+                lora_copies[i].start()
+
+    z_copies = {}
+    for piece, dzs in enumerate(steps):
+        for k in (1, 2, 3):
+            lora_copies[piece * LEVEL + k].wait_recv()
+        terms = lora_in[piece * LEVEL : (piece + 1) * LEVEL].reshape(LEVEL * 2 * CAP, width)
+        for pos, dz in enumerate(dzs):
+            t = total[(z + dz) % levels] + mm(place[pos], terms)
+            if dz == 0:
+                result = t
+            else:
+                z_out[dz] = t.astype(BF16)
+                z_copies[dz] = send(
+                    z_out.at[dz], z_in.at[dz], z_s.at[dz], z_r.at[dz], device(dz, 0, 0)
+                )
+                z_copies[dz].start()
     for dz in range(1, levels):
         z_copies[dz].wait_recv()
         result = result + z_in[dz].astype(F32)
     out[...] = result.astype(out.dtype)
 
+    far_copy.wait_send()
+    for j in range(1, side):
+        near_copies[j].wait_send()
+        relay_copies[j].wait_send()
     for k in range(1, parts):
-        pack_copies[k].wait_send()
+        direct_copies[k].wait_send()
     for i in range(2 * levels):
         core_copy(i).wait_send()
     for i in range(levels):
         y_copy(i).wait_send()
-    for k in (1, 2, 3):
-        lora_copies[k].wait_send()
+    for i in lora_copies:
+        lora_copies[i].wait_send()
     for dz in range(1, levels):
         z_copies[dz].wait_send()
 
@@ -214,7 +265,9 @@
     rows, depth = hidden.shape
     features = down_weight.shape[1]
     width = features // parts
-    rank = adapter_down.shape[0]
+    relayed = depth // 256 * 4 // 7 * 256
+    direct = depth - relayed
+    side = parts // 2
     vmem = pl.BlockSpec(memory_space=pltpu.VMEM)
     anywhere = pl.BlockSpec(memory_space=pl.ANY)
     dma = pltpu.SemaphoreType.DMA
@@ -228,22 +281,31 @@
             pltpu.VMEM(adapter_down.shape, BF16),
             pltpu.VMEM(adapter_up.shape, BF16),
             pltpu.VMEM((parts, CAP, rows), F32),
-            pltpu.VMEM((parts, 2 * CAP, depth // 2), BF16),
-            pltpu.VMEM((parts, 2 * CAP, depth // 2), BF16),
+            pltpu.VMEM((2, rows, LEVEL * 2 * CAP), BF16),
+            pltpu.VMEM((rows, relayed), BF16),
+            pltpu.VMEM((side, 2 * CAP, relayed // 2), BF16),
+            pltpu.VMEM((side, 2 * CAP, relayed // 2), BF16),
+            pltpu.VMEM((side, 2 * CAP, relayed // 2), BF16),
+            pltpu.VMEM((side, 2 * CAP, relayed // 2), BF16),
+            pltpu.VMEM((parts, 2 * CAP, direct // 2), BF16),
+            pltpu.VMEM((parts, 2 * CAP, direct // 2), BF16),
             pltpu.VMEM((2 * levels, rows, width), F32),
             pltpu.VMEM((2 * levels, rows, width), F32),
             pltpu.VMEM((levels, rows, width), BF16),
             pltpu.VMEM((levels, rows, width), BF16),
             pltpu.VMEM((levels, rows, width), F32),
-            pltpu.VMEM((LEVEL, levels * CAP, width), BF16),
-            pltpu.VMEM((LEVEL, levels * CAP, width), BF16),
+            pltpu.VMEM((2 * LEVEL, 2 * CAP, width), BF16),
+            pltpu.VMEM((2 * LEVEL, 2 * CAP, width), BF16),
             pltpu.VMEM((levels, rows, width), BF16),
             pltpu.VMEM((levels, rows, width), BF16),
             dma((parts,)), dma, dma,
+            dma, dma,
+            dma((side,)), dma((side,)),
+            dma((side,)), dma((side,)),
             dma((parts,)), dma((parts,)),
             dma((2 * levels,)), dma((2 * levels,)),
             dma((levels,)), dma((levels,)),
-            dma((LEVEL,)), dma((LEVEL,)),
+            dma((2 * LEVEL,)), dma((2 * LEVEL,)),
             dma((levels,)), dma((levels,)),
         ],
         compiler_params=pltpu.CompilerParams(
@@ -286,7 +348,7 @@
 ):
     parts = lax.axis_size("tp")
     tiled = (
-        parts % LEVEL == 0
+        parts == 4 * LEVEL
         and hidden.shape[1] % 256 == 0
         and down_weight.shape[1] % (128 * parts) == 0
         and hidden.shape[0] == 128

time: 61.6 us -> 56.8 us (0.922)
  Pallas kernels: 59.9 us -> 55 us
    pallas_call x1, Pallas kernels: 59.9 us -> 55 us  [fused(): pl.pallas_call(functools.partial(kernel, levels), out_shape=jax.ShapeDtyp...]
where the time goes in v2:
time: 56.8 us; the launch traced here: 56.6 us
  Pallas kernels  55 us (97%)
  local copies, waits for them, and re-layouts  1.57 us (3%)
    pallas_call x1, Pallas kernels, fused(): pl.pallas_call(functools.partial(kernel, levels), out_shape=jax.ShapeDtyp...  55 us
    unnamed x1, local copies, waits for them, and re-layouts  1.57 us

profile of v2, /device:TPU:0, one launch (start us, length us, event | category | flops | bytes accessed | tf_op | source)
XLA Modules:
  0.0 56.6 jit_solution(16509413448933673979)
XLA Ops:
  0.0 55.0 %shard_map.64 = bf16[128,512]{1,0:T(8,128)(2,1)} custom-call(bf16[128,1792]{1,0:T(8,128)(2,1)} %hid.1, s32[1,128]{1,0:T(1,128)} %bitcast.6, s32[1,16]{1,0:T(1,128)} %bitcast.7, bf16[1792,8192]{1,0:T(8,128)(2,1)} %down_hbm.1, bf16[64,28672]{1,0:T(8,128)(2,1)} %bitcast.4, bf16[64,8192]{1,0:T(8,128)(2,1)} %bitcast.5), custom_call_target="tpu_custom_call" | custom-call | flops 3758096384 | bytes 29360128 | tf_op jit(solution)/shard_map/pallas_call | solution.py:274
  55.0 1.6 %copy.8 = bf16[128,512]{1,0:T(8,128)(2,1)} copy(bf16[128,512]{1,0:T(8,128)(2,1)} %shard_map.64) | data formatting | bytes 262144

commit v3 on v2

--- a/solution.py
+++ b/solution.py
@@ -19,9 +19,9 @@
 
 def kernel(
     levels, hid, ids, holder, down_hbm, a_hbm, u_hbm, out,
-    w, a, u, sel, place, far, near_out, near_in, relay_out, relay_in, direct_out, direct_in,
+    w, a, u, sel, place, far, aside, near_out, near_in, relay_out, relay_in, direct_out, direct_in,
     core_out, core_in, y_out, y_in, total, lora_out, lora_in, z_out, z_in,
-    w_sem, a_sem, u_sem, far_s, far_r, near_s, near_r, relay_s, relay_r, direct_s, direct_r,
+    w_sem, a_sem, u_sem, far_s, far_r, aside_s, aside_r, near_s, near_r, relay_s, relay_r, direct_s, direct_r,
     core_s, core_r, y_s, y_r, lora_s, lora_r, z_s, z_r,
 ):
     parts = levels * LEVEL
@@ -92,6 +92,8 @@
     pl.semaphore_wait(barrier, parts - 1)
     far_copy = send(hid.at[:, pl.ds(0, relayed)], far, far_s, far_r, device(levels // 2, 0, 0))
     far_copy.start()
+    aside_copy = send(hid.at[:, pl.ds(relayed, depth - relayed)], aside, aside_s, aside_r, device(0, 1, 0))
+    aside_copy.start()
 
     def pack(first, groups, x, to):
         def body(i, carry):
@@ -112,15 +114,6 @@
     ]
     for j in range(side - 1, 0, -1):
         near_copies[j].start()
-    pack(0, levels, lambda: hid[:, relayed:], direct_out)
-    direct_copies = [
-        send(direct_out.at[device(*offsets[k])], direct_in.at[k], direct_s.at[k], direct_r.at[k],
-             device(*offsets[k]))
-        for k in range(parts)
-    ]
-    for k in range(parts - 1, 0, -1):
-        direct_copies[k].start()
-
     def core_copy(i):
         return send(core_out.at[i], core_in.at[i], core_s.at[i], core_r.at[i], device(0, 0, 1))
 
@@ -149,12 +142,33 @@
         t = product(3, zz)
         core_copy(levels + zz).wait_recv()
         t = t + core_in[levels + zz]
-        y_copy(zz).wait_recv()
-        total[zz] = t + y_in[zz].astype(F32)
+        total[zz] = t
         return carry
 
     to_core(0, 0)
     lax.fori_loop(0, levels, to_y, 0)
+    aside_copy.wait_recv()
+
+    def pack_direct(i, carry):
+        s = sel[pl.ds(i * 4 + y * 2, 2)].reshape(2 * CAP, rows).astype(BF16)
+        t = mm(s, hid[:, relayed:])
+        v = mm(s, aside[...])
+        for j in range(2):
+            at = slice(j * CAP, (j + 1) * CAP)
+            direct_out[i * 2 + j] = jnp.concatenate([t[at], v[at]], axis=0).astype(BF16)
+        return carry
+
+    lax.fori_loop(0, levels, pack_direct, 0)
+    direct_copies = []
+    for k in range(side):
+        dev = device(k // 2, 0, k % 2)
+        direct_copies.append(
+            send(direct_out.at[dev // 4 * 2 + dev % 2], direct_in.at[k], direct_s.at[k],
+                 direct_r.at[k], dev)
+        )
+    for k in range(side - 1, 0, -1):
+        direct_copies[k].start()
+
     to_core(levels, 2)
 
     far_copy.wait_recv()
@@ -191,14 +205,28 @@
         return t0[:CAP] + t1[CAP:]
 
     low = down_map(near_out[inner(0)], me * depth)
-    low += down_map(direct_out[me], me * depth + relayed)
+
+    def direct_map(x, src, pair):
+        dims = (((1,), (1,)), ((), ()))
+        n = x.shape[1]
+        t0 = lax.dot_general(
+            x, a[:, pl.ds(pl.multiple_of(src * depth + relayed, 128), n)], dims,
+            preferred_element_type=F32,
+        )
+        t1 = lax.dot_general(
+            x, a[:, pl.ds(pl.multiple_of(pair * depth + relayed, 128), n)], dims,
+            preferred_element_type=F32,
+        )
+        return t0[:CAP] + t1[CAP:]
+
+    low += direct_map(direct_out[z * 2 + c], me, device(0, 1, 0))
     low += down_map(relay_out[inner(0)], ((1 - half) * side + inner(0)) * depth)
     for j in range(1, side):
         near_copies[j].wait_recv()
         low += down_map(near_in[j], (half * side + inner(j)) * depth)
-    for k in range(1, parts):
+    for k in range(1, side):
         direct_copies[k].wait_recv()
-        low += down_map(direct_in[k], back(*offsets[k]) * depth + relayed)
+        low += direct_map(direct_in[k], back(k // 2, 0, k % 2), back(k // 2, 1, k % 2))
     for j in range(1, side):
         relay_copies[j].wait_recv()
         low += down_map(relay_in[j], ((1 - half) * side + inner(j)) * depth)
@@ -229,7 +257,9 @@
             lora_copies[piece * LEVEL + k].wait_recv()
         terms = lora_in[piece * LEVEL : (piece + 1) * LEVEL].reshape(LEVEL * 2 * CAP, width)
         for pos, dz in enumerate(dzs):
-            t = total[(z + dz) % levels] + mm(place[pos], terms)
+            zz = (z + dz) % levels
+            y_copy(zz).wait_recv()
+            t = total[zz] + y_in[zz].astype(F32) + mm(place[pos], terms)
             if dz == 0:
                 result = t
             else:
@@ -247,7 +277,8 @@
     for j in range(1, side):
         near_copies[j].wait_send()
         relay_copies[j].wait_send()
-    for k in range(1, parts):
+    aside_copy.wait_send()
+    for k in range(1, side):
         direct_copies[k].wait_send()
     for i in range(2 * levels):
         core_copy(i).wait_send()
@@ -283,12 +314,13 @@
             pltpu.VMEM((parts, CAP, rows), F32),
             pltpu.VMEM((2, rows, LEVEL * 2 * CAP), BF16),
             pltpu.VMEM((rows, relayed), BF16),
+            pltpu.VMEM((rows, direct), BF16),
             pltpu.VMEM((side, 2 * CAP, relayed // 2), BF16),
             pltpu.VMEM((side, 2 * CAP, relayed // 2), BF16),
             pltpu.VMEM((side, 2 * CAP, relayed // 2), BF16),
             pltpu.VMEM((side, 2 * CAP, relayed // 2), BF16),
-            pltpu.VMEM((parts, 2 * CAP, direct // 2), BF16),
-            pltpu.VMEM((parts, 2 * CAP, direct // 2), BF16),
+            pltpu.VMEM((side, 2 * CAP, direct), BF16),
+            pltpu.VMEM((side, 2 * CAP, direct), BF16),
             pltpu.VMEM((2 * levels, rows, width), F32),
             pltpu.VMEM((2 * levels, rows, width), F32),
             pltpu.VMEM((levels, rows, width), BF16),
@@ -300,9 +332,10 @@
             pltpu.VMEM((levels, rows, width), BF16),
             dma((parts,)), dma, dma,
             dma, dma,
+            dma, dma,
             dma((side,)), dma((side,)),
             dma((side,)), dma((side,)),
-            dma((parts,)), dma((parts,)),
+            dma((side,)), dma((side,)),
             dma((2 * levels,)), dma((2 * levels,)),
             dma((levels,)), dma((levels,)),
             dma((2 * LEVEL,)), dma((2 * LEVEL,)),

time: 56.8 us -> 52.8 us (0.930)
  Pallas kernels: 55 us -> 51 us
    pallas_call x1, Pallas kernels: 55 us -> 51 us  [fused(): pl.pallas_call(functools.partial(kernel, levels), out_shape=jax.ShapeDtyp...]
where the time goes in v3:
time: 52.8 us; the launch traced here: 52.6 us
  Pallas kernels  51 us (97%)
  local copies, waits for them, and re-layouts  1.57 us (3%)
    pallas_call x1, Pallas kernels, fused(): pl.pallas_call(functools.partial(kernel, levels), out_shape=jax.ShapeDtyp...  51 us
    unnamed x1, local copies, waits for them, and re-layouts  1.57 us

profile of v3, /device:TPU:0, one launch (start us, length us, event | category | flops | bytes accessed | tf_op | source)
XLA Modules:
  0.0 52.6 jit_solution(6939797744589338520)
XLA Ops:
  0.0 51.0 %shard_map.64 = bf16[128,512]{1,0:T(8,128)(2,1)} custom-call(bf16[128,1792]{1,0:T(8,128)(2,1)} %hid.1, s32[1,128]{1,0:T(1,128)} %bitcast.6, s32[1,16]{1,0:T(1,128)} %bitcast.7, bf16[1792,8192]{1,0:T(8,128)(2,1)} %down_hbm.1, bf16[64,28672]{1,0:T(8,128)(2,1)} %bitcast.4, bf16[64,8192]{1,0:T(8,128)(2,1)} %bitcast.5), custom_call_target="tpu_custom_call" | custom-call | flops 3758096384 | bytes 29360128 | tf_op jit(solution)/shard_map/pallas_call | solution.py:305
  51.1 1.6 %copy.8 = bf16[128,512]{1,0:T(8,128)(2,1)} copy(bf16[128,512]{1,0:T(8,128)(2,1)} %shard_map.64) | data formatting | bytes 262144

commit v4 on v3

--- a/solution.py
+++ b/solution.py
@@ -61,11 +61,11 @@
         )
 
     barrier = pltpu.get_barrier_semaphore()
-    offsets = [(k // 4, (k // 2) % 2, k % 2) for k in range(parts)]
-    for k in range(1, parts):
+    peers = [device(k // 2, 0, k % 2) for k in range(side - 1, 0, -1)]
+    peers += [half * side + inner(j) for j in range(side) if j // 2 % 2 == 1]
+    for peer in peers:
         pl.semaphore_signal(
-            barrier, inc=1, device_id={"tp": device(*offsets[k])},
-            device_id_type=pl.DeviceIdType.MESH,
+            barrier, inc=1, device_id={"tp": peer}, device_id_type=pl.DeviceIdType.MESH
         )
     for p in range(4):
         for zz in range(levels):
@@ -89,7 +89,7 @@
             slot[o : o + 1, :] == lax.broadcasted_iota(jnp.int32, (CAP, rows), 0)
         ).astype(F32)
 
-    pl.semaphore_wait(barrier, parts - 1)
+    pl.semaphore_wait(barrier, len(peers))
     far_copy = send(hid.at[:, pl.ds(0, relayed)], far, far_s, far_r, device(levels // 2, 0, 0))
     far_copy.start()
     aside_copy = send(hid.at[:, pl.ds(relayed, depth - relayed)], aside, aside_s, aside_r, device(0, 1, 0))

time: 52.8 us -> 52.7 us (level)
  no operation moved by 1% of the time
where the time goes in v4:
time: 52.7 us; the launch traced here: 52.5 us
  Pallas kernels  50.9 us (97%)
  local copies, waits for them, and re-layouts  1.57 us (3%)
    pallas_call x1, Pallas kernels, fused(): pl.pallas_call(functools.partial(kernel, levels), out_shape=jax.ShapeDtyp...  50.9 us
    unnamed x1, local copies, waits for them, and re-layouts  1.57 us

profile of v4, /device:TPU:0, one launch (start us, length us, event | category | flops | bytes accessed | tf_op | source)
XLA Modules:
  0.0 52.5 jit_solution(8019731081531580818)
XLA Ops:
  0.0 50.9 %shard_map.64 = bf16[128,512]{1,0:T(8,128)(2,1)} custom-call(bf16[128,1792]{1,0:T(8,128)(2,1)} %hid.1, s32[1,128]{1,0:T(1,128)} %bitcast.6, s32[1,16]{1,0:T(1,128)} %bitcast.7, bf16[1792,8192]{1,0:T(8,128)(2,1)} %down_hbm.1, bf16[64,28672]{1,0:T(8,128)(2,1)} %bitcast.4, bf16[64,8192]{1,0:T(8,128)(2,1)} %bitcast.5), custom_call_target="tpu_custom_call" | custom-call | flops 3758096384 | bytes 29360128 | tf_op jit(solution)/shard_map/pallas_call | solution.py:305
  51.0 1.6 %copy.8 = bf16[128,512]{1,0:T(8,128)(2,1)} copy(bf16[128,512]{1,0:T(8,128)(2,1)} %shard_map.64) | data formatting | bytes 262144
